TPU v7x, 32 devices: a whole 2x2x4 slice. The times are simulated.
32 devices in a mesh: re: 16 (over z, y, core), kq: 2 (over x).
Axes of the slice: x: 2, y: 2, z: 4, core: 2. Of those that a mesh axis runs over, the one named last changes fastest.
Arguments:
- couplings: bfloat16 [2, 64, 2, 18, 1024], P(None, 're'), may hold values from -0.41992188 to 0.41992188
- re_vectors: int32 [64, 3], P('re'), may hold values from -8 to 8
- degeneracy: int32 [64], P('re'), may hold values from 1 to 8
- kpoints: int32 [64, 3], P('kq'), may hold values from 0 to 15
- plus_index: int32 [64, 2], P('kq'), may hold values from 0 to 63, as said below
- mode_vectors: float32 [2, 2, 18, 18], replicated, may hold values from -1 to 1
- band_vectors: float32 [64, 2, 32, 16], P('kq'), may hold values from -0.75 to 0.75
Outputs:
- rotated_couplings: float32 [2, 16, 72, 512], P('kq', 're')
Inputs may be any that keep to these rules, and one draw needn't show every extreme that they name: `plus_index`: each column lists every one of the 64 fine k points exactly once.
All inputs are finite; a program needn't handle non-finite values.
Results may differ from a plain program's by a relative error of at most 0.0023.
Values may be sent and summed in bfloat16 or wider, within the bound.
A program may use at most 128 MiB of HBM per device.

v0:
```python
import math

import jax
import jax.numpy as jnp
from jax import lax
from jax.sharding import PartitionSpec as P

W = 32
NB = 16
M = 18
Q = 2
NG = 16


precise = lax.Precision.HIGHEST


def phase_matrix(kint, rint, degen):
    product = jnp.sum(kint[:, None, :] * rint[None, :, :], axis=-1)
    angle = jnp.mod(product, NG).astype(jnp.float32) * (2.0 * math.pi / NG)
    weight = 1.0 / degen.astype(jnp.float32)
    cosine = jnp.cos(angle) * weight[None, :]
    sine = jnp.sin(angle) * weight[None, :]
    upper = jnp.concatenate([cosine, -sine], axis=1)
    lower = jnp.concatenate([sine, cosine], axis=1)
    return jnp.concatenate([upper, lower], axis=0).astype(jnp.bfloat16)


def phase_sum(kint, rint, degen, values):
    phases = phase_matrix(kint, rint, degen)
    lattice_count = values.shape[1]
    stacked = values.reshape(2 * lattice_count, -1)
    bloch = jnp.dot(phases, stacked, preferred_element_type=jnp.float32)
    return bloch.reshape(2, kint.shape[0], Q, M, -1)


def rotate_modes(real_part, imag_part, vectors):
    er = vectors[:, 0]
    ei = vectors[:, 1]
    out_real = jnp.einsum("qvu,kqvx->kqux", er, real_part, precision=precise) - jnp.einsum(
        "qvu,kqvx->kqux", ei, imag_part, precision=precise
    )
    out_imag = jnp.einsum("qvu,kqvx->kqux", er, imag_part, precision=precise) + jnp.einsum(
        "qvu,kqvx->kqux", ei, real_part, precision=precise
    )
    return (out_real, out_imag)


def project_right(real_part, imag_part, factor):
    fr = factor[:, 0]
    fi = factor[:, 1]
    out_real = jnp.einsum("rmn,rnj->rmj", real_part, fr, precision=precise) - jnp.einsum(
        "rmn,rnj->rmj", imag_part, fi, precision=precise
    )
    out_imag = jnp.einsum("rmn,rnj->rmj", real_part, fi, precision=precise) + jnp.einsum(
        "rmn,rnj->rmj", imag_part, fr, precision=precise
    )
    return jnp.stack([out_real, out_imag], axis=1)


def project_left(values, factor):
    fr = factor[:, 0]
    fi = factor[:, 1]
    xr = values[:, 0]
    xi = values[:, 1]
    out_real = jnp.einsum("rmi,rmj->rij", fr, xr, precision=precise) + jnp.einsum(
        "rmi,rmj->rij", fi, xi, precision=precise
    )
    out_imag = jnp.einsum("rmi,rmj->rij", fr, xi, precision=precise) - jnp.einsum(
        "rmi,rmj->rij", fi, xr, precision=precise
    )
    return jnp.stack([out_real, out_imag], axis=1)


def plus_bands(plus_index, band_vectors, pair_ids):
    targets = plus_index[pair_ids // Q, pair_ids % Q]
    every_band = lax.all_gather(band_vectors, "kq", axis=0, tiled=True)
    return every_band[targets]


def shards(couplings, re_vectors, degeneracy, kpoints, plus_index, mode_vectors, band_vectors):
    local_count = kpoints.shape[0]
    local_rows = local_count * Q * M
    share_rows = local_rows // lax.axis_size("re")
    share_pairs = share_rows // M
    share_ids = lax.axis_index("re") * share_rows + jnp.arange(share_rows, dtype=jnp.int32)
    pair_share = lax.axis_index("re") * share_pairs + jnp.arange(share_pairs, dtype=jnp.int32)
    local_share = jnp.arange(share_rows, dtype=jnp.int32) // M
    moved = lax.all_to_all(couplings, "re", split_axis=4, concat_axis=1, tiled=True)
    lattice_all, degen_all = (
        lax.all_gather(re_vectors, "re", axis=0, tiled=True),
        lax.all_gather(degeneracy, "re", axis=0, tiled=True),
    )
    columns = moved.shape[4]
    bloch = phase_sum(kpoints, lattice_all, degen_all, moved)
    moded_real, moded_imag = rotate_modes(bloch[0], bloch[1], mode_vectors)
    paired = jnp.stack([moded_real, moded_imag]).reshape(2, local_rows, columns)
    returned = lax.all_to_all(paired, "re", split_axis=1, concat_axis=2, tiled=True)
    right = project_right(
        returned[0].reshape(share_rows, W, W),
        returned[1].reshape(share_rows, W, W),
        band_vectors[share_ids // (Q * M)],
    )
    fetched = plus_bands(plus_index, band_vectors, pair_share)
    result = project_left(right, fetched[local_share])
    return result.reshape(1, 1, share_rows, 2 * NB * NB)


def solution(mesh):
    return jax.shard_map(
        shards,
        mesh=mesh,
        in_specs=(
            P(None, "re", None, None, None),
            P("re", None),
            P("re"),
            P("kq", None),
            P("kq", None),
            P(),
            P("kq", None, None, None),
        ),
        out_specs=P("kq", "re", None, None),
        check_vma=False,
    )
```

profile of v0, /device:TPU:0, one launch (start us, length us, event | category | flops | bytes accessed | tf_op | source)
XLA Modules:
  0.0 145.9 jit_solution(15561041977517925938)
XLA Ops:
  0.0 7.1 %copy.92 = bf16[2,4,2,18,1024]{3,1,2,0,4:T(4,128)(2,1)} copy(bf16[2,4,2,18,1024]{4,2,3,1,0:T(2,128)(2,1)} %param.7) | data formatting | bytes 1179648 | tf_op args[0]
  7.1 8.7 %reshape.251 = bf16[16,2,9216]{2,1,0:T(2,128)(2,1)} reshape(bf16[1024,2,2,4,18]{4,3,2,1,0:T(4,128)(2,1)} %bitcast.83) | data formatting | bytes 1179648
  15.9 7.5 %all-to-all-start = ((bf16[16,2,9216]{2,1,0:T(2,128)(2,1)}), bf16[16,2,9216]{2,1,0:T(2,128)(2,1)S(1)}, u32[]{:S(2)}, u32[]{:S(2)}) async-start(bf16[16,2,9216]{2,1,0:T(2,128)(2,1)} %reshape.251), calls=%async_computation | async-start | bytes 1179648 | tf_op jit(solution)/shard_map/all_to_all | solution.py:89
  23.4 26.2 %all-gather = s32[16,4,3]{2,1,0:T(4,128)S(1)} all-gather(s32[1,4,3]{2,1,0:T(4,128)S(1)} %bitcast.93), channel_id=1, replica_groups=mesh['re'=16,'kq'=2] {'re'}, dimensions={0}, use_global_device_ids=true | all-gather | bytes 816 | tf_op jit(solution)/shard_map/all_gather | solution.py:91
  49.7 0.1 copy.120
  49.8 0.1 copy.121
  49.9 0.6 dynamic-slice
  51.2 0.2 dynamic-update-slice
  51.4 9.9 %all-reduce = s32[64]{0:T(128)S(1)} all-reduce(s32[64]{0:T(128)S(1)} %dynamic-update-slice), channel_id=1, replica_groups=mesh['re'=16,'kq'=2] {'re'}, use_global_device_ids=true, to_apply=%add | all-reduce | flops 64 | bytes 512
  61.4 0.1 negate_convert_fusion
  61.6 11.4 %reshape.252 = bf16[1024,2,2,4,18]{4,3,2,1,0:T(4,128)(2,1)} reshape(bf16[16,2,9216]{2,1,0:T(2,128)(2,1)S(1)} %all-to-all-done) | data formatting | bytes 1179648
  73.0 6.4 %copy.93 = bf16[2,4,2,18,16,64]{5,3,2,1,4,0:T(8,128)(2,1)S(1)} copy(bf16[2,4,2,18,16,64]{3,1,2,0,5,4:T(4,128)(2,1)} %bitcast.84) | data formatting | bytes 1179648 | tf_op jit(solution)/shard_map/all_to_all | solution.py:89
  79.4 0.9 reshape.210
  80.3 0.3 fusion.21
  80.7 0.2 squeeze.25
  80.9 0.2 squeeze.27
  81.2 0.8 fusion.8
  82.0 0.8 fusion.4
  82.8 0.8 fusion.1
  83.7 0.8 fusion
  84.7 4.3 %copy.134 = f32[2,1152,64]{2,0,1:T(2,128)S(1)} copy(f32[2,1152,64]{2,1,0:T(8,128)S(1)} %pad_maximum_fusion) | data formatting | bytes 1179648 | tf_op jit(solution)/shard_map/stack | solution.py:97
  89.0 2.1 %reshape.253 = f32[16,1,9216]{2,1,0:T(1,128)} reshape(f32[1152,2,64]{2,1,0:T(2,128)S(1)} %bitcast.86) | data formatting | bytes 1179648
  91.1 4.4 %all-to-all-start.1 = ((f32[16,1,9216]{2,1,0:T(1,128)}), f32[16,1,9216]{2,1,0:T(1,128)S(1)}, u32[]{:S(2)}, u32[]{:S(2)}) async-start(f32[16,1,9216]{2,1,0:T(1,128)} %reshape.253), calls=%async_computation.1 | async-start | bytes 1179648 | tf_op jit(solution)/shard_map/all_to_all | solution.py:98
  95.6 0.7 gather_fusion.3
  96.3 0.6 gather_fusion
  96.9 15.3 %all_gather.9 = f32[64,2,32,16]{2,3,1,0:T(8,128)} all-gather(f32[32,2,32,16]{2,3,1,0:T(8,128)S(1)} %copy-done.1), channel_id=1, replica_groups=mesh['re'=16,'kq'=2] {'kq'}, dimensions={0}, use_global_device_ids=true | all-gather | bytes 393216 | tf_op jit(solution)/shard_map/all_gather | solution.py:77
  112.2 1.8 %gather_fusion.1 = f32[4,2,32,16]{2,3,1,0:T(8,128)S(1)} fusion(f32[64,2,32,16]{2,3,1,0:T(8,128)} %all_gather.9, s32[1024]{0:T(1024)S(1)} %pad_clamp_fusion.2), kind=kCustom, calls=%fused_computation.1 | custom fusion | bytes 32784 | tf_op jit(solution)/shard_map/gather | solution.py:78
  114.0 0.7 gather_fusion.2
  114.7 0.5 broadcast.307
  115.2 3.0 %reduce = f32[16,9216]{1,0:T(8,128)} reduce(f32[16,1,9216]{2,1,0:T(1,128)S(1)} %all-to-all-done.1, f32[]{:T(128)} %broadcast.307), dimensions={1}, to_apply=%all_to_all.25.reduce_sub_computation | reduce | bytes 1179652 | tf_op jit(solution)/shard_map/all_to_all | solution.py:98
  118.2 1.9 %reshape.254 = f32[1152,2,64]{2,1,0:T(2,128)S(1)} reshape(f32[16,9216]{1,0:T(8,128)} %reduce) | data formatting | bytes 1179648
  120.1 1.4 copy.118
  121.5 2.1 %fusion.40 = (f32[1,72,16,64]{1,2,3,0:T(8,128)}, f32[1,72,16,64]{1,2,3,0:T(8,128)S(1)}) fusion(f32[2,72,16,64]{1,2,3,0:T(8,128)} %bitcast.88), kind=kLoop, calls=%fused_computation.82 | loop fusion | bytes 1179648 | tf_op jit(solution)/shard_map/slice | solution.py:101
  123.6 1.0 copy.104
  124.5 2.1 %copy.106 = f32[72,32,32]{2,1,0:T(8,128)S(1)} copy(f32[72,32,32]{0,2,1:T(8,128)} %bitcast.89) | data formatting | bytes 589824 | tf_op jit(solution)/shard_map/reshape;squeeze | solution.py:100
  126.6 2.8 %fusion.12 = f32[72,32,16]{1,2,0:T(8,128)} fusion(f32[72,32,32]{2,1,0:T(8,128)S(1)} %copy.106, f32[72,2,32,16]{2,3,1,0:T(8,128)S(1)} %gather_fusion.3), kind=kOutput, calls=%fused_computation.27 | convolution fusion | flops 14155776 | bytes 1916928 | tf_op jit(solution)/shard_map/rmn,rnj->rmj/dot_general | solution.py:52
  129.4 2.8 %fusion.13 = f32[72,32,16]{1,2,0:T(8,128)} fusion(f32[72,32,32]{2,1,0:T(8,128)S(1)} %copy.106, f32[72,2,32,16]{2,3,1,0:T(8,128)S(1)} %gather_fusion.3), kind=kOutput, calls=%fused_computation.28 | convolution fusion | flops 14155776 | bytes 1916928 | tf_op jit(solution)/shard_map/rmn,rnj->rmj/dot_general | solution.py:55
  132.2 1.0 copy.107
  133.1 2.1 %copy.109 = f32[72,32,32]{2,1,0:T(8,128)S(1)} copy(f32[72,32,32]{0,2,1:T(8,128)} %bitcast.90) | data formatting | bytes 589824 | tf_op jit(solution)/shard_map/reshape;squeeze | solution.py:101
  135.2 3.1 %convolution_subtract_fusion.2 = f32[72,32,16]{1,2,0:T(8,128)S(1)} fusion(f32[72,32,16]{1,2,0:T(8,128)} %fusion.12, f32[72,32,32]{2,1,0:T(8,128)S(1)} %copy.109, f32[72,2,32,16]{2,3,1,0:T(8,128)S(1)} %gather_fusion.3), kind=kOutput, calls=%fused_computation.13 | convolution fusion | flops 14192640 | bytes 2064384 | tf_op jit(solution)/shard_map/rmn,rnj->rmj/dot_general | solution.py:52
  138.3 2.0 %convolution_add_fusion.2 = f32[72,32,16]{1,2,0:T(8,128)S(1)} fusion(f32[72,32,16]{1,2,0:T(8,128)S(1)} %copy-done.4, f32[72,32,32]{2,1,0:T(8,128)S(1)} %copy.109, f32[72,2,32,16]{2,3,1,0:T(8,128)S(1)} %gather_fusion.3), kind=kOutput, calls=%fused_computation.12 | convolution fusion | flops 14192640 | bytes 2506752 | tf_op jit(solution)/shard_map/rmn,rnj->rmj/dot_general | solution.py:55
  140.3 1.1 fusion.11
  141.4 1.1 fusion.10
  142.4 1.1 fusion.2
  143.5 0.3 copy.113
  143.8 1.1 fusion.3
  144.8 0.3 copy.114
  145.1 0.8 copy.115
  (43 shorter events, 0.7 us)
Async XLA Ops:
  0.0 96.2 %copy-start = (s32[32,2]{0,1:T(2,128)S(1)}, s32[32,2]{0,1:T(2,128)}, u32[]{:S(2)}) copy-start(s32[32,2]{0,1:T(2,128)} %param.11) | copy-start | bytes 772
  15.8 7.6 %copy-start.7 = (s32[4,3]{1,0:T(4,128)S(1)}, s32[4,3]{1,0:T(4,128)}, u32[]{:S(2)}) copy-start(s32[4,3]{1,0:T(4,128)} %param.8) | copy-start | bytes 148
  15.8 33.8 %copy-start.6 = (f32[2,2,18,18]{3,1,2,0:T(2,128)S(1)}, f32[2,2,18,18]{3,1,2,0:T(2,128)}, u32[]{:S(2)}) copy-start(f32[2,2,18,18]{3,1,2,0:T(2,128)} %param.12) | copy-start | bytes 15556
  15.8 34.1 %copy-start.10 = (u32[32]{0:T(128)S(1)}, u32[32]{0:T(128)}, u32[]{:S(2)}) copy-start(u32[32]{0:T(128)} %constant.96) | copy-start | bytes 388
  15.8 35.3 %copy-start.9 = (s32[4]{0:T(128)S(1)}, s32[4]{0:T(128)}, u32[]{:S(2)}) copy-start(s32[4]{0:T(128)} %param.9) | copy-start | bytes 52
  15.8 45.5 %copy-start.8 = (s32[32,3]{0,1:T(4,128)S(1)}, s32[32,3]{0,1:T(4,128)}, u32[]{:S(2)}) copy-start(s32[32,3]{0,1:T(4,128)} %param.10) | copy-start | bytes 1156
  15.9 45.7 %all-to-all-start = ((bf16[16,2,9216]{2,1,0:T(2,128)(2,1)}), bf16[16,2,9216]{2,1,0:T(2,128)(2,1)S(1)}, u32[]{:S(2)}, u32[]{:S(2)}) async-start(bf16[16,2,9216]{2,1,0:T(2,128)(2,1)} %reshape.251), calls=%async_computation | async-start | bytes 1179648 | tf_op jit(solution)/shard_map/all_to_all | solution.py:89
  89.0 6.6 %copy-start.1 = (f32[32,2,32,16]{2,3,1,0:T(8,128)S(1)}, f32[32,2,32,16]{2,3,1,0:T(8,128)}, u32[]{:S(2)}) copy-start(f32[32,2,32,16]{2,3,1,0:T(8,128)} %param.13) | copy-start | bytes 393220
  91.1 23.6 %all-to-all-start.1 = ((f32[16,1,9216]{2,1,0:T(1,128)}), f32[16,1,9216]{2,1,0:T(1,128)S(1)}, u32[]{:S(2)}, u32[]{:S(2)}) async-start(f32[16,1,9216]{2,1,0:T(1,128)} %reshape.253), calls=%async_computation.1 | async-start | bytes 1179648 | tf_op jit(solution)/shard_map/all_to_all | solution.py:98
  129.4 2.8 %copy-start.5 = (f32[1,72,16,64]{1,2,3,0:T(8,128)S(1)}, f32[1,72,16,64]{1,2,3,0:T(8,128)}, u32[]{:S(2)}) copy-start(f32[1,72,16,64]{1,2,3,0:T(8,128)} %get-tuple-element.5) | copy-start | bytes 884740
  135.2 3.1 %copy-start.4 = (f32[72,32,16]{1,2,0:T(8,128)S(1)}, f32[72,32,16]{1,2,0:T(8,128)}, u32[]{:S(2)}) copy-start(f32[72,32,16]{1,2,0:T(8,128)} %fusion.13) | copy-start | bytes 442372
  138.3 2.0 %copy-start.2 = (f32[72,32,16]{1,2,0:T(8,128)}, f32[72,32,16]{1,2,0:T(8,128)S(1)}, u32[]{:S(2)}) copy-start(f32[72,32,16]{1,2,0:T(8,128)S(1)} %convolution_subtract_fusion.2) | copy-start | bytes 442372
  142.4 1.3 copy-start.3
where the time goes:
time: 147 us; the launch traced here: 146 us
  local copies, waits for them, and re-layouts  60 us (41%)
  blocking collectives  51.4 us (35%)
  matrix products  18.2 us (12%)
  starting transfers between devices  11.9 us (8%)
  other arithmetic  3.35 us (2%)
    unnamed x33, local copies, waits for them, and re-layouts  32.4 us
    all_gather x1, blocking collectives, shards(): lax.all_gather(re_vectors, 're', axis=0, tiled=True)  26.2 us
    all_gather x1, blocking collectives, plus_bands(): every_band = lax.all_gather(band_vectors, 'kq', axis=0, tiled=True)  15.3 us
    unnamed x1, blocking collectives  9.93 us
    all_to_all x1, starting transfers between devices, shards(): lax.all_to_all(couplings, 're', split_axis=4, concat_axis=1, tiled=True)  7.53 us
    all_to_all x1, local copies, waits for them, and re-layouts, shards(): lax.all_to_all(couplings, 're', split_axis=4, concat_axis=1, tiled=True)  6.44 us
    another operation x3, local copies, waits for them, and re-layouts, shards(): paired = jnp.stack([moded_real, moded_imag]).reshape(2, local_rows, columns)  4.4 us
    all_to_all x1, starting transfers between devices, shards(): lax.all_to_all(paired, 're', split_axis=1, concat_axis=2, tiled=True)  4.4 us
  transfers between devices with their start and end apart: 2, of which 0 were waited for; matrix products, arithmetic and copies ran while one was open for 4% of the time, Pallas kernels for 0%

commit v1 on v0

--- a/solution.py
+++ b/solution.py
@@ -1,8 +1,11 @@
+import functools
 import math
 
 import jax
 import jax.numpy as jnp
 from jax import lax
+from jax.experimental import pallas as pl
+from jax.experimental.pallas import tpu as pltpu
 from jax.sharding import PartitionSpec as P
 
 W = 32
@@ -106,9 +109,332 @@
     return result.reshape(1, 1, share_rows, 2 * NB * NB)
 
 
+MESH = pl.DeviceIdType.MESH
+LANES = 640
+GEO = 576
+f32 = jnp.float32
+bf16 = jnp.bfloat16
+NT = (((1,), (1,)), ((), ()))
+TN = (((0,), (0,)), ((), ()))
+
+
+def iota(shape, axis):
+    return lax.broadcasted_iota(jnp.int32, shape, axis)
+
+
+def exact(a, b, dims=(((1,), (0,)), ((), ()))):
+    return lax.dot_general(a, b, dims, precision=precise, preferred_element_type=f32)
+
+
+def split(a):
+    high = a.astype(bf16)
+    return high, (a - high.astype(f32)).astype(bf16)
+
+
+def dot16(a, b):
+    return jnp.dot(a, b, preferred_element_type=f32)
+
+
+def unit_cosine(step):
+    step = step - NG * jnp.floor(step * (1.0 / NG))
+    fold = jnp.minimum(step, NG - step)
+    near = jnp.minimum(fold, 8.0 - fold)
+    size = jnp.where(near < 0.5, 1.0, jnp.where(near < 1.5, math.cos(math.pi / 8), math.cos(math.pi / 4)))
+    size = jnp.where(near > 2.5, math.cos(3 * math.pi / 8), size)
+    size = jnp.where(near > 3.5, 0.0, size)
+    return jnp.where(fold > 4.5, -size, size)
+
+
+def quarter_swap(parts):
+    lane = iota(parts[0].shape, 1)
+    upper = (lane & 64) != 0
+    odd = (lane & 32) != 0
+    stage = list(parts)
+    for a, b in ((0, 2), (1, 3)):
+        moved = pltpu.roll(jnp.where(upper, parts[a], parts[b]), 64, 1)
+        stage[a] = jnp.where(upper, moved, parts[a])
+        stage[b] = jnp.where(upper, parts[b], moved)
+    out = list(stage)
+    for a, b in ((0, 1), (2, 3)):
+        out[a] = jnp.where(odd, pltpu.roll(stage[b], 32, 1), stage[a])
+        out[b] = jnp.where(odd, stage[b], pltpu.roll(stage[a], 96, 1))
+    return out
+
+
+def group_swap(x):
+    sub = iota(x.shape, 0)
+    group = iota(x.shape, 1) // 16
+    rows = x.shape[0]
+    for s in (4, 2, 1):
+        low_a = (sub & s) == 0
+        low_b = (group & s) == 0
+        down = pltpu.roll(pltpu.roll(x, rows - s, 0), 16 * s, 1)
+        up = pltpu.roll(pltpu.roll(x, s, 0), 128 - 16 * s, 1)
+        x = jnp.where(low_a == low_b, x, jnp.where(low_a, down, up))
+    return x
+
+
+def unpack_bands(tile):
+    return jnp.concatenate([tile] + [pltpu.roll(tile, 128 - 32 * g, 1) for g in (1, 2, 3)], axis=0)
+
+
+def kernel(
+    n_re, n_kq, coup, geo, kp, bz, mode, plus, out,
+    F, Y, X, S, D, BZ, KP, send1, recv1, send2, recv2, sendb, recvb,
+):
+    re = lax.axis_index("re")
+    kq = lax.axis_index("kq")
+    n_all = n_re * n_kq
+    me = kq * n_re + re
+    barrier = pltpu.get_barrier_semaphore()
+
+    def hello(off, carry):
+        to = lax.rem(me + off, n_all)
+        pl.semaphore_signal(
+            barrier, inc=1, device_id=(lax.rem(to, n_re), to // n_re), device_id_type=MESH
+        )
+        return carry
+
+    lax.fori_loop(1, n_all, hello, 0)
+
+    width = n_re * W
+    tiles = width // 128
+    for a in range(16):
+        c, r, q = a // 8, (a // 2) % 4, a % 2
+        for t in range(tiles):
+            lanes = pl.ds(pl.multiple_of(kq * width + t * 128, 128), 128)
+            F[t, a * 24 : a * 24 + M, :] = coup[c, r, q, :, lanes].astype(f32)
+    spare = geo[...]
+    for t in range(tiles):
+        for v4 in range(5):
+            parts = []
+            for v in range(4 * v4, 4 * v4 + 4):
+                if v < M:
+                    parts.append(F[t, pl.ds(v, 16, stride=24), :])
+                else:
+                    parts.append(jnp.zeros((16, 128), f32))
+            moved = quarter_swap(parts)
+            for m in range(4):
+                piece = moved[m] + spare if v4 == 4 else moved[m]
+                Y[t * 4 + m, :, v4 * 128 : v4 * 128 + 128] = piece.astype(bf16)
+
+    pl.semaphore_wait(barrier, n_all - 1)
+
+    def first(to, frm):
+        return pltpu.make_async_remote_copy(
+            src_ref=Y.at[to], dst_ref=X.at[frm],
+            send_sem=send1.at[to], recv_sem=recv1.at[frm],
+            device_id=(to, kq), device_id_type=MESH,
+        )
+
+    def swap(ref, full, s, off):
+        other = lax.rem(kq + off, n_kq)
+        return pltpu.make_async_remote_copy(
+            src_ref=ref, dst_ref=full.at[kq],
+            send_sem=sendb.at[s, other], recv_sem=recvb.at[s, kq],
+            device_id=(re, other), device_id_type=MESH,
+        )
+
+    def swapped(ref, full, s, off):
+        other = lax.rem(kq + off, n_kq)
+        return pltpu.make_async_remote_copy(
+            src_ref=ref, dst_ref=full.at[other],
+            send_sem=sendb.at[s, other], recv_sem=recvb.at[s, other],
+            device_id=(re, other), device_id_type=MESH,
+        )
+
+    for off in range(1, n_kq):
+        swap(kp, KP, 0, off).start()
+
+    def go1(off, carry):
+        first(lax.rem(re + off, n_re), re).start()
+        return carry
+
+    lax.fori_loop(1, n_re, go1, 0)
+    for off in range(1, n_kq):
+        swap(bz, BZ, 1, off).start()
+    X[re] = Y[re]
+    KP[kq] = kp[...]
+    BZ[kq] = bz[...]
+    for off in range(1, n_kq):
+        swapped(kp, KP, 0, off).wait_recv()
+    n_k = n_kq * kp.shape[0]
+    rows = n_k * 4
+    pick = ((iota((rows, n_k), 0) // 4) == iota((rows, n_k), 1)).astype(bf16)
+    grid = dot16(pick, KP[...].reshape(n_k, 128).astype(bf16)).astype(bf16)
+
+    def got1(off, carry):
+        first(re, lax.rem(re + off, n_re)).wait_recv()
+        return carry
+
+    lax.fori_loop(1, n_re, got1, 0)
+    depth = n_re * 16
+    lattice = X[:, :, 512:640].reshape(depth, 128)
+    product = lax.dot_general(grid, lattice, NT, preferred_element_type=f32)
+    ones = (iota((rows, 128), 1) == 67).astype(bf16)
+    degen = lax.dot_general(ones, lattice, NT, preferred_element_type=f32)
+    row = iota((rows, depth), 0)
+    col = iota((rows, depth), 1)
+    turn = (((col // 8) & 1) - (row & 1)).astype(f32) * 4.0
+    same = ((row // 2) & 1) == (col & 1)
+    phases = jnp.where(same, unit_cosine(product + turn) * (1.0 / degen), 0.0).astype(bf16)
+    for t in range(5):
+        lanes = slice(t * 128, t * 128 + 128)
+        bloch = dot16(phases, X[:, :, lanes].reshape(depth, 128))
+        S[:, :, lanes] = bloch.reshape(n_all, 8, 128).astype(bf16)
+
+    def second(to, frm):
+        return pltpu.make_async_remote_copy(
+            src_ref=S.at[to], dst_ref=D.at[frm],
+            send_sem=send2.at[to], recv_sem=recv2.at[frm],
+            device_id=(lax.rem(to, n_re), to // n_re), device_id_type=MESH,
+        )
+
+    def go2(off, carry):
+        second(lax.rem(me + off, n_all), me).start()
+        return carry
+
+    lax.fori_loop(1, n_all, go2, 0)
+    D[me] = S[me]
+
+    for off in range(1, n_kq):
+        swapped(bz, BZ, 1, off).wait_recv()
+    spread = (iota((128, 256), 0) == iota((128, 256), 1) // 8).astype(f32)
+    lane = iota((NB, 256), 1)
+    imag_in = (lane & 1) == 1
+    left = []
+    for p in range(4):
+        target = plus[re * 2 + p // 2, p % 2]
+        n_dev = kp.shape[0]
+        tile = BZ[target // n_dev, lax.rem(target, n_dev)]
+        wide = exact(unpack_bands(tile), spread)
+        real, imag = wide[:NB], wide[NB:]
+        mine = ((lane // 2) & 3) == p
+        left.append(jnp.where(mine, jnp.where(imag_in, imag, real), 0.0))
+        left.append(jnp.where(mine, jnp.where(imag_in, real, -imag), 0.0))
+    left_high, left_low = split(jnp.concatenate(left, axis=0))
+    left_both = jnp.concatenate([left_high, left_low], axis=0)
+    down = ((iota((256, 128), 0) & 31) == iota((256, 128), 1)).astype(f32)
+    lane = iota((32, 256), 1)
+    across = iota((32, 256), 0) == (lane // 128) * NB + (lane & 15)
+    flip = iota((32, 256), 0) == (1 - lane // 128) * NB + (lane & 15)
+    minus = jnp.where(lane < 128, -1.0, 1.0)
+    same_mode = iota((256, 256), 0) // 32 == (iota((256, 256), 1) // NB) % 8
+    right = []
+    for k in range(2):
+        tall = exact(down, unpack_bands(bz[re * 2 + k]), NT)
+        a = exact(tall, across.astype(f32))
+        b = exact(tall, jnp.where(flip, minus, 0.0))
+        right.append([split(jnp.where(same_mode, w, 0.0)) for w in (a, b)])
+
+    def got2(off, carry):
+        second(me, lax.rem(me + off, n_all)).wait_recv()
+        return carry
+
+    lax.fori_loop(1, n_all, got2, 0)
+    data = D[...].astype(f32).reshape(n_all * 8, LANES).astype(bf16)
+    both = dot16(left_both, data)
+    summed = both[:128] + both[128:]
+    groups = [
+        summed[:, 0:256],
+        summed[:, 256:512],
+        jnp.concatenate([summed[:, 512:640], jnp.zeros((128, 128), f32)], axis=1),
+    ]
+    values = [[None, None], [None, None]]
+    for k in range(2):
+        total = None
+        for c in range(2):
+            x = jnp.concatenate(
+                [g[((k * 2 + q) * 2 + c) * NB : ((k * 2 + q) * 2 + c + 1) * NB] for g in groups for q in range(2)],
+                axis=0,
+            )
+            high, low = split(x)
+            w_high, w_low = right[k][c]
+            term = dot16(high, w_high) + dot16(low, w_high) + dot16(high, w_low)
+            total = term if total is None else total + term
+        for c in range(2):
+            turned = group_swap(total[:, c * 128 : c * 128 + 128])
+            for q in range(2):
+                values[q][c] = (values[q][c] or []) + [
+                    jnp.concatenate(
+                        [
+                            jnp.concatenate(
+                                [turned[(g * 2 + q) * NB + h * 8 : (g * 2 + q) * NB + h * 8 + 8] for g in range(3)],
+                                axis=0,
+                            )
+                            for h in range(2)
+                        ],
+                        axis=1,
+                    )
+                ]
+    for q in range(2):
+        xr = jnp.concatenate(values[q][0], axis=1)[:M]
+        xi = jnp.concatenate(values[q][1], axis=1)[:M]
+        er, ei = mode[q, 0], mode[q, 1]
+        yr = exact(er, xr, TN) - exact(ei, xi, TN)
+        yi = exact(er, xi, TN) + exact(ei, xr, TN)
+        for k in range(2):
+            at = (k * 2 + q) * M
+            out[0, 0, at : at + M, 0:256] = yr[:, k * 256 : k * 256 + 256]
+            out[0, 0, at : at + M, 256:512] = yi[:, k * 256 : k * 256 + 256]
+
+    for off in range(1, n_kq):
+        swap(kp, KP, 0, off).wait_send()
+        swap(bz, BZ, 1, off).wait_send()
+
+    def sent1(off, carry):
+        first(lax.rem(re + off, n_re), re).wait_send()
+        return carry
+
+    lax.fori_loop(1, n_re, sent1, 0)
+
+    def sent2(off, carry):
+        second(lax.rem(me + off, n_all), me).wait_send()
+        return carry
+
+    lax.fori_loop(1, n_all, sent2, 0)
+
+
+def fused(n_re, n_kq, couplings, re_vectors, degeneracy, kpoints, plus_index, mode_vectors, band_vectors):
+    n_all = n_re * n_kq
+    k_dev = kpoints.shape[0]
+    lattice = jnp.concatenate([re_vectors, degeneracy[:, None]], axis=1).astype(f32)
+    lattice = jnp.broadcast_to(lattice[None, :, None, :], (2, 4, 2, 4)).reshape(16, 4)
+    geo = jnp.pad(lattice, ((0, 0), (64, 60)))
+    kp = jnp.pad(kpoints.astype(f32), ((0, 0), (64, 61)))
+    bz = band_vectors.transpose(0, 1, 3, 2).reshape(k_dev, 4, 8, W).transpose(0, 2, 1, 3).reshape(k_dev, 8, 128)
+    vmem = pl.BlockSpec(memory_space=pltpu.VMEM)
+    return pl.pallas_call(
+        functools.partial(kernel, n_re, n_kq),
+        out_shape=jax.ShapeDtypeStruct((1, 1, k_dev * Q * M // n_re, 2 * NB * NB), f32),
+        in_specs=[vmem] * 5 + [pl.BlockSpec(memory_space=pltpu.SMEM)],
+        out_specs=vmem,
+        scratch_shapes=[
+            pltpu.VMEM((n_re * W // 128, 16 * 24, 128), f32),
+            pltpu.VMEM((n_re, 16, LANES), bf16),
+            pltpu.VMEM((n_re, 16, LANES), bf16),
+            pltpu.VMEM((n_all, 8, LANES), bf16),
+            pltpu.VMEM((n_all, 8, LANES), bf16),
+            pltpu.VMEM((n_kq, k_dev, 8, 128), f32),
+            pltpu.VMEM((n_kq, k_dev, 128), f32),
+            pltpu.SemaphoreType.DMA((n_re,)),
+            pltpu.SemaphoreType.DMA((n_re,)),
+            pltpu.SemaphoreType.DMA((n_all,)),
+            pltpu.SemaphoreType.DMA((n_all,)),
+            pltpu.SemaphoreType.DMA((2, n_kq)),
+            pltpu.SemaphoreType.DMA((2, n_kq)),
+        ],
+        compiler_params=pltpu.CompilerParams(
+            collective_id=0, has_side_effects=True, vmem_limit_bytes=48 * 1024 * 1024
+        ),
+    )(couplings, geo, kp, bz, mode_vectors, plus_index)
+
+
 def solution(mesh):
+    n_re, n_kq = mesh.shape["re"], mesh.shape["kq"]
+    body = functools.partial(fused, n_re, n_kq) if (n_re, n_kq) == (NB, W // NB) else shards
     return jax.shard_map(
-        shards,
+        body,
         mesh=mesh,
         in_specs=(
             P(None, "re", None, None, None),

time: 147 us -> 33.3 us (0.23)
  local copies, waits for them, and re-layouts: 60 us -> 5.36 us
  blocking collectives: 51.4 us -> 0 us
  Pallas kernels: 0 us -> 27.5 us
  matrix products: 18.2 us -> 0 us
  starting transfers between devices: 11.9 us -> 0 us
  other arithmetic: 3.35 us -> 0.08 us
    all_gather x2 -> x0, blocking collectives: 41.4 us -> none  [the longest x1 26.2 us: shards(): lax.all_gather(re_vectors, 're', axis=0, tiled=True)]
    unnamed x33 -> x16, local copies, waits for them, and re-layouts: 32.4 us -> 3.59 us
    pallas_call x0 -> x1, Pallas kernels: none -> 27.5 us  [fused(): pl.pallas_call(functools.partial(kernel, n_re, n_kq), out_shape=jax.Shape...]
    dot_general x13 -> x0, matrix products: 18.2 us -> none  [the longest x1 3.09 us: project_right(): jnp.einsum('rmn,rnj->rmj', imag_part, fi, precision=precise)]
    all_to_all x2 -> x0, starting transfers between devices: 11.9 us -> none  [the longest x1 7.53 us: shards(): lax.all_to_all(couplings, 're', split_axis=4, concat_axis=1, tiled=True)]
    unnamed x1 -> x0, blocking collectives: 9.93 us -> none
    another operation x7 -> x0, local copies, waits for them, and re-layouts: 9.1 us -> none  [the longest x3 4.4 us: shards(): paired = jnp.stack([moded_real, moded_imag]).reshape(2, local_rows, columns)]
    all_to_all x3 -> x0, local copies, waits for them, and re-layouts: 8.32 us -> none  [the longest x1 6.44 us: shards(): lax.all_to_all(couplings, 're', split_axis=4, concat_axis=1, tiled=True)]
  transfers between devices with their start and end apart: 2 -> 0, of which waited for: 0 -> 0; matrix products, arithmetic and copies ran while one was open for 4% -> 0% of each run, Pallas kernels for 0% -> 0%
where the time goes in v1:
time: 33.3 us; the launch traced here: 33 us
  Pallas kernels  27.5 us (83%)
  local copies, waits for them, and re-layouts  5.36 us (16%)
    pallas_call x1, Pallas kernels, fused(): pl.pallas_call(functools.partial(kernel, n_re, n_kq), out_shape=jax.Shape...  27.5 us
    unnamed x16, local copies, waits for them, and re-layouts  3.59 us
    reshape x2, local copies, waits for them, and re-layouts, fused(): band_vectors.transpose(0, 1, 3, 2).reshape(k_dev, 4, 8, W)  1.43 us

profile of v1, /device:TPU:0, one launch (start us, length us, event | category | flops | bytes accessed | tf_op | source)
XLA Modules:
  0.0 33.0 jit_solution(7464744384647596940)
XLA Ops:
  0.0 0.0 copy-start.5
  0.0 0.0 copy-start.2
  0.0 0.7 %copy-done.5 = s32[4]{0:T(128)S(1)} copy-done((s32[4]{0:T(128)S(1)}, s32[4]{0:T(128)}, u32[]{:S(2)}) %copy-start.5) | copy-done | bytes 40
  0.7 0.1 copy.14
  0.7 0.0 copy-done.2
  0.8 0.0 copy-start.3
  0.8 0.1 add_convert_fusion
  0.8 0.6 %copy-done.3 = s32[32,3]{0,1:T(4,128)S(1)} copy-done((s32[32,3]{0,1:T(4,128)S(1)}, s32[32,3]{0,1:T(4,128)}, u32[]{:S(2)}) %copy-start.3) | copy-done | bytes 408
  1.4 0.1 pad.8.geo
  1.5 0.0 copy-start.1
  1.5 0.1 copy.15
  1.6 0.0 copy-start.4
  1.6 0.1 pad.9.kp
  1.7 0.6 %copy-done.4 = s32[32,2]{0,1:T(2,128)S(1)} copy-done((s32[32,2]{0,1:T(2,128)S(1)}, s32[32,2]{0,1:T(2,128)}, u32[]{:S(2)}) %copy-start.4) | copy-done | bytes 280
  2.3 0.1 copy.19.plus
  2.4 0.0 copy-done.1
  2.4 1.2 %copy.21 = f32[32,4,8,32]{3,1,2,0:T(4,128)S(1)} copy(f32[32,4,8,32]{3,2,1,0:T(8,128)} %bitcast.9) | data formatting | bytes 262144 | tf_op jit(solution)/shard_map/reshape | solution.py:405
  3.6 0.0 copy-start
  3.6 0.3 reshape.27.bz
  3.8 0.8 %copy-done = bf16[2,4,2,18,1024]{4,2,3,1,0:T(2,128)(2,1)S(1)} copy-done((bf16[2,4,2,18,1024]{4,2,3,1,0:T(2,128)(2,1)S(1)}, bf16[2,4,2,18,1024]{4,2,3,1,0:T(2,128)(2,1)}, u32[]{:S(2)}) %copy-start) | copy-done | bytes 589848
  4.6 0.2 copy.17.coup
  4.8 27.5 %shard_map.73 = f32[1,1,72,512]{3,2,1,0:T(8,128)S(1)} custom-call(bf16[2,4,2,18,1024]{4,3,2,1,0:T(8,128)(2,1)S(1)} %copy.17.coup, f32[16,128]{1,0:T(8,128)S(1)} %pad.8.geo, f32[32,128]{1,0:T(8,128)S(1)} %pad.9.kp, f32[32,8,128]{2,1,0:T(8,128)S(1)} %reshape.27.bz, f32[2,2,18,18]{3,2,1,0:T(8,128)S(1)} %copy.18.mode, s32[32,2]{1,0:T(8,128)S(1)} %copy.19.plus), custom_call_target="tpu_custom_call" | custom-call | tf_op jit(solution)/shard_map/pallas_call | solution.py:407
  32.3 0.7 %copy.23 = f32[1,1,72,512]{3,2,1,0:T(8,128)} copy(f32[1,1,72,512]{3,2,1,0:T(8,128)S(1)} %shard_map.73) | data formatting | bytes 294912
  (3 shorter events, 0.0 us)
Async XLA Ops:
  0.0 0.7 %copy-start.5 = (s32[4]{0:T(128)S(1)}, s32[4]{0:T(128)}, u32[]{:S(2)}) copy-start(s32[4]{0:T(128)} %param.9) | copy-start | bytes 52
  0.0 0.7 %copy-start.2 = (s32[4,3]{1,0:T(4,128)S(1)}, s32[4,3]{1,0:T(4,128)}, u32[]{:S(2)}) copy-start(s32[4,3]{1,0:T(4,128)} %param.8) | copy-start | bytes 148
  0.8 0.7 %copy-start.3 = (s32[32,3]{0,1:T(4,128)S(1)}, s32[32,3]{0,1:T(4,128)}, u32[]{:S(2)}) copy-start(s32[32,3]{0,1:T(4,128)} %param.10) | copy-start | bytes 1156
  1.5 0.9 %copy-start.1 = (f32[2,2,18,18]{3,1,2,0:T(2,128)S(1)}, f32[2,2,18,18]{3,1,2,0:T(2,128)}, u32[]{:S(2)}) copy-start(f32[2,2,18,18]{3,1,2,0:T(2,128)} %param.12) | copy-start | bytes 15556
  1.6 0.7 %copy-start.4 = (s32[32,2]{0,1:T(2,128)S(1)}, s32[32,2]{0,1:T(2,128)}, u32[]{:S(2)}) copy-start(s32[32,2]{0,1:T(2,128)} %param.11) | copy-start | bytes 772
  3.6 1.1 %copy-start = (bf16[2,4,2,18,1024]{4,2,3,1,0:T(2,128)(2,1)S(1)}, bf16[2,4,2,18,1024]{4,2,3,1,0:T(2,128)(2,1)}, u32[]{:S(2)}) copy-start(bf16[2,4,2,18,1024]{4,2,3,1,0:T(2,128)(2,1)} %param.7) | copy-start | bytes 1769476

commit v2 on v1

--- a/solution.py
+++ b/solution.py
@@ -179,13 +179,29 @@
 
 
 def kernel(
-    n_re, n_kq, coup, geo, kp, bz, mode, plus, out,
-    F, Y, X, S, D, BZ, KP, send1, recv1, send2, recv2, sendb, recvb,
+    n_re, n_kq, coup_any, rvec_any, degen_any, kp_any, plus_any, mode_any, bands_any, out,
+    coup, rvec, degen_own, kp_own, plus, mode, bands,
+    F, Y, X, S, D, BZ, KP, bz, kp, fetch, send1, recv1, send2, recv2, sendb, recvb,
 ):
     re = lax.axis_index("re")
     kq = lax.axis_index("kq")
     n_all = n_re * n_kq
     me = kq * n_re + re
+    width = n_re * W
+    tiles = width // 128
+    mine = pl.ds(pl.multiple_of(kq * width, width), width)
+    pairs = [
+        (coup_any.at[:, :, :, :, mine], coup),
+        (rvec_any, rvec),
+        (degen_any, degen_own),
+        (kp_any, kp_own),
+        (bands_any, bands),
+        (plus_any, plus),
+        (mode_any, mode),
+    ]
+    loads = [pltpu.make_async_copy(a, b, fetch.at[n]) for n, (a, b) in enumerate(pairs)]
+    for load in loads:
+        load.start()
     barrier = pltpu.get_barrier_semaphore()
 
     def hello(off, carry):
@@ -197,22 +213,24 @@
 
     lax.fori_loop(1, n_all, hello, 0)
 
-    width = n_re * W
-    tiles = width // 128
-    for a in range(16):
-        c, r, q = a // 8, (a // 2) % 4, a % 2
-        for t in range(tiles):
-            lanes = pl.ds(pl.multiple_of(kq * width + t * 128, 128), 128)
-            F[t, a * 24 : a * 24 + M, :] = coup[c, r, q, :, lanes].astype(f32)
-    spare = geo[...]
+    for n in range(4):
+        loads[n].wait()
+    kp[...] = jnp.zeros_like(kp)
+    kp[0:3, 0 : kp_own.shape[1]] = kp_own[...].astype(f32)
+    row = iota((16, 128), 0) // 2 % 4
+    lane = iota((16, 128), 1)
+    spare = jnp.zeros((16, 128), f32)
+    for r in range(4):
+        for d in range(4):
+            value = (rvec[r, d] if d < 3 else degen_own[r]).astype(f32)
+            spare = jnp.where((row == r) & (lane == 64 + d), value, spare)
     for t in range(tiles):
+        for a in range(8):
+            F[t, :, 2 * a : 2 * a + 2, :] = coup[a // 4, a % 4, :, :, t * 128 : t * 128 + 128].astype(f32)
         for v4 in range(5):
             parts = []
             for v in range(4 * v4, 4 * v4 + 4):
-                if v < M:
-                    parts.append(F[t, pl.ds(v, 16, stride=24), :])
-                else:
-                    parts.append(jnp.zeros((16, 128), f32))
+                parts.append(F[t, v] if v < M else jnp.zeros((16, 128), f32))
             moved = quarter_swap(parts)
             for m in range(4):
                 piece = moved[m] + spare if v4 == 4 else moved[m]
@@ -251,17 +269,26 @@
         return carry
 
     lax.fori_loop(1, n_re, go1, 0)
+    loads[4].wait()
+    for g in range(4):
+        bz[:, :, g * 32 : g * 32 + 32] = bands[:, g // 2, g % 2 * 8 : g % 2 * 8 + 8, :]
     for off in range(1, n_kq):
         swap(bz, BZ, 1, off).start()
+    loads[5].wait()
+    loads[6].wait()
     X[re] = Y[re]
     KP[kq] = kp[...]
     BZ[kq] = bz[...]
     for off in range(1, n_kq):
         swapped(kp, KP, 0, off).wait_recv()
-    n_k = n_kq * kp.shape[0]
-    rows = n_k * 4
-    pick = ((iota((rows, n_k), 0) // 4) == iota((rows, n_k), 1)).astype(bf16)
-    grid = dot16(pick, KP[...].reshape(n_k, 128).astype(bf16)).astype(bf16)
+    n_dev = bz.shape[0]
+    rows = n_kq * n_dev * 4
+    points = KP[0]
+    for other in range(1, n_kq):
+        points = points + pltpu.roll(KP[other], other * n_dev, 1)
+    points = jnp.concatenate([jnp.zeros((64, 128), f32), points, jnp.zeros((56, 128), f32)], axis=0)
+    pick = ((iota((rows, 128), 0) // 4) == iota((rows, 128), 1)).astype(bf16)
+    grid = lax.dot_general(pick, points.astype(bf16), NT, preferred_element_type=f32).astype(bf16)
 
     def got1(off, carry):
         first(re, lax.rem(re + off, n_re)).wait_recv()
@@ -304,14 +331,13 @@
     imag_in = (lane & 1) == 1
     left = []
     for p in range(4):
-        target = plus[re * 2 + p // 2, p % 2]
-        n_dev = kp.shape[0]
+        target = plus[p % 2, re * 2 + p // 2]
         tile = BZ[target // n_dev, lax.rem(target, n_dev)]
         wide = exact(unpack_bands(tile), spread)
         real, imag = wide[:NB], wide[NB:]
-        mine = ((lane // 2) & 3) == p
-        left.append(jnp.where(mine, jnp.where(imag_in, imag, real), 0.0))
-        left.append(jnp.where(mine, jnp.where(imag_in, real, -imag), 0.0))
+        own = ((lane // 2) & 3) == p
+        left.append(jnp.where(own, jnp.where(imag_in, imag, real), 0.0))
+        left.append(jnp.where(own, jnp.where(imag_in, real, -imag), 0.0))
     left_high, left_low = split(jnp.concatenate(left, axis=0))
     left_both = jnp.concatenate([left_high, left_low], axis=0)
     down = ((iota((256, 128), 0) & 31) == iota((256, 128), 1)).astype(f32)
@@ -370,7 +396,7 @@
     for q in range(2):
         xr = jnp.concatenate(values[q][0], axis=1)[:M]
         xi = jnp.concatenate(values[q][1], axis=1)[:M]
-        er, ei = mode[q, 0], mode[q, 1]
+        er, ei = mode[q, :, 0, :], mode[q, :, 1, :]
         yr = exact(er, xr, TN) - exact(ei, xi, TN)
         yi = exact(er, xi, TN) + exact(ei, xr, TN)
         for k in range(2):
@@ -398,25 +424,30 @@
 def fused(n_re, n_kq, couplings, re_vectors, degeneracy, kpoints, plus_index, mode_vectors, band_vectors):
     n_all = n_re * n_kq
     k_dev = kpoints.shape[0]
-    lattice = jnp.concatenate([re_vectors, degeneracy[:, None]], axis=1).astype(f32)
-    lattice = jnp.broadcast_to(lattice[None, :, None, :], (2, 4, 2, 4)).reshape(16, 4)
-    geo = jnp.pad(lattice, ((0, 0), (64, 60)))
-    kp = jnp.pad(kpoints.astype(f32), ((0, 0), (64, 61)))
-    bz = band_vectors.transpose(0, 1, 3, 2).reshape(k_dev, 4, 8, W).transpose(0, 2, 1, 3).reshape(k_dev, 8, 128)
     vmem = pl.BlockSpec(memory_space=pltpu.VMEM)
     return pl.pallas_call(
         functools.partial(kernel, n_re, n_kq),
         out_shape=jax.ShapeDtypeStruct((1, 1, k_dev * Q * M // n_re, 2 * NB * NB), f32),
-        in_specs=[vmem] * 5 + [pl.BlockSpec(memory_space=pltpu.SMEM)],
+        in_specs=[pl.BlockSpec(memory_space=pltpu.HBM)] * 7,
         out_specs=vmem,
         scratch_shapes=[
-            pltpu.VMEM((n_re * W // 128, 16 * 24, 128), f32),
+            pltpu.VMEM((2, 4, M, Q, n_re * W), bf16),
+            pltpu.SMEM((4, 3), jnp.int32),
+            pltpu.SMEM((4,), jnp.int32),
+            pltpu.VMEM((3, k_dev), jnp.int32),
+            pltpu.SMEM((Q, k_dev), jnp.int32),
+            pltpu.VMEM((Q, M, 2, M), f32),
+            pltpu.VMEM((k_dev, 2, NB, W), f32),
+            pltpu.VMEM((n_re * W // 128, M, 16, 128), f32),
             pltpu.VMEM((n_re, 16, LANES), bf16),
             pltpu.VMEM((n_re, 16, LANES), bf16),
             pltpu.VMEM((n_all, 8, LANES), bf16),
             pltpu.VMEM((n_all, 8, LANES), bf16),
             pltpu.VMEM((n_kq, k_dev, 8, 128), f32),
-            pltpu.VMEM((n_kq, k_dev, 128), f32),
+            pltpu.VMEM((n_kq, 8, 128), f32),
+            pltpu.VMEM((k_dev, 8, 128), f32),
+            pltpu.VMEM((8, 128), f32),
+            pltpu.SemaphoreType.DMA((7,)),
             pltpu.SemaphoreType.DMA((n_re,)),
             pltpu.SemaphoreType.DMA((n_re,)),
             pltpu.SemaphoreType.DMA((n_all,)),
@@ -425,9 +456,17 @@
             pltpu.SemaphoreType.DMA((2, n_kq)),
         ],
         compiler_params=pltpu.CompilerParams(
-            collective_id=0, has_side_effects=True, vmem_limit_bytes=48 * 1024 * 1024
+            collective_id=0, has_side_effects=True, vmem_limit_bytes=60 * 1024 * 1024
         ),
-    )(couplings, geo, kp, bz, mode_vectors, plus_index)
+    )(
+        couplings.transpose(0, 1, 3, 2, 4),
+        re_vectors,
+        degeneracy,
+        kpoints.T,
+        plus_index.T,
+        mode_vectors.transpose(0, 2, 1, 3),
+        band_vectors.transpose(0, 1, 3, 2),
+    )
 
 
 def solution(mesh):

time: 33.3 us -> 29.1 us (0.87)
  local copies, waits for them, and re-layouts: 5.36 us -> 1.58 us
    unnamed x16 -> x1, local copies, waits for them, and re-layouts: 3.59 us -> 1.58 us
    reshape x2 -> x0, local copies, waits for them, and re-layouts: 1.43 us -> none  [fused(): band_vectors.transpose(0, 1, 3, 2).reshape(k_dev, 4, 8, W)]
where the time goes in v2:
time: 29.1 us; the launch traced here: 29 us
  Pallas kernels  27.4 us (94%)
  local copies, waits for them, and re-layouts  1.58 us (5%)
    pallas_call x1, Pallas kernels, fused(): pl.pallas_call(functools.partial(kernel, n_re, n_kq), out_shape=jax.Shape...  27.4 us
    unnamed x1, local copies, waits for them, and re-layouts  1.58 us

profile of v2, /device:TPU:0, one launch (start us, length us, event | category | flops | bytes accessed | tf_op | source)
XLA Modules:
  0.0 29.0 jit_solution(7109601070568922020)
XLA Ops:
  0.0 27.4 %shard_map.73 = f32[1,1,72,512]{3,2,1,0:T(8,128)} custom-call(bf16[2,4,18,2,1024]{4,3,2,1,0:T(2,128)(2,1)} %bitcast.5, s32[4,3]{1,0:T(4,128)} %rvec_any.1, s32[4]{0:T(128)} %degen_any.1, s32[3,32]{1,0:T(4,128)} %bitcast.8, s32[2,32]{1,0:T(2,128)} %bitcast.9, f32[2,18,2,18]{3,2,1,0:T(2,128)} %bitcast.7, f32[32,2,16,32]{3,2,1,0:T(8,128)} %bitcast.6), custom_call_target="tpu_custom_call" | custom-call | tf_op jit(solution)/shard_map/pallas_call | solution.py:428
  27.4 1.6 %copy.9 = f32[1,1,72,512]{3,2,1,0:T(8,128)} copy(f32[1,1,72,512]{3,2,1,0:T(8,128)} %shard_map.73) | data formatting | bytes 294912

commit v3 on v2

--- a/solution.py
+++ b/solution.py
@@ -111,7 +111,8 @@
 
 MESH = pl.DeviceIdType.MESH
 LANES = 640
-GEO = 576
+QUADS = ((4, 0, 1), (2, 3))
+CHUNKS = ((0, 384), (384, 256))
 f32 = jnp.float32
 bf16 = jnp.bfloat16
 NT = (((1,), (1,)), ((), ()))
@@ -224,24 +225,11 @@
         for d in range(4):
             value = (rvec[r, d] if d < 3 else degen_own[r]).astype(f32)
             spare = jnp.where((row == r) & (lane == 64 + d), value, spare)
-    for t in range(tiles):
-        for a in range(8):
-            F[t, :, 2 * a : 2 * a + 2, :] = coup[a // 4, a % 4, :, :, t * 128 : t * 128 + 128].astype(f32)
-        for v4 in range(5):
-            parts = []
-            for v in range(4 * v4, 4 * v4 + 4):
-                parts.append(F[t, v] if v < M else jnp.zeros((16, 128), f32))
-            moved = quarter_swap(parts)
-            for m in range(4):
-                piece = moved[m] + spare if v4 == 4 else moved[m]
-                Y[t * 4 + m, :, v4 * 128 : v4 * 128 + 128] = piece.astype(bf16)
-
-    pl.semaphore_wait(barrier, n_all - 1)
-
-    def first(to, frm):
+    def first(to, frm, part):
+        lanes = pl.ds(*CHUNKS[part])
         return pltpu.make_async_remote_copy(
-            src_ref=Y.at[to], dst_ref=X.at[frm],
-            send_sem=send1.at[to], recv_sem=recv1.at[frm],
+            src_ref=Y.at[to, :, lanes], dst_ref=X.at[frm, :, lanes],
+            send_sem=send1.at[part, to], recv_sem=recv1.at[part, frm],
             device_id=(to, kq), device_id_type=MESH,
         )
 
@@ -261,14 +249,30 @@
             device_id=(re, other), device_id_type=MESH,
         )
 
-    for off in range(1, n_kq):
-        swap(kp, KP, 0, off).start()
-
-    def go1(off, carry):
-        first(lax.rem(re + off, n_re), re).start()
-        return carry
-
-    lax.fori_loop(1, n_re, go1, 0)
+    for part, quads in enumerate(QUADS):
+        for t in range(tiles):
+            for v4 in quads:
+                count = min(4, M - 4 * v4)
+                for a in range(8):
+                    F[t, 4 * v4 : 4 * v4 + count, 2 * a : 2 * a + 2, :] = coup[
+                        a // 4, a % 4, 4 * v4 : 4 * v4 + count, :, t * 128 : t * 128 + 128
+                    ].astype(f32)
+                parts = [F[t, 4 * v4 + v] if v < count else jnp.zeros((16, 128), f32) for v in range(4)]
+                moved = quarter_swap(parts)
+                at = (v4 + 1) % 5 * 128
+                for m in range(4):
+                    piece = moved[m] + spare if v4 == 4 else moved[m]
+                    Y[t * 4 + m, :, at : at + 128] = piece.astype(bf16)
+        if part == 0:
+            pl.semaphore_wait(barrier, n_all - 1)
+            for off in range(1, n_kq):
+                swap(kp, KP, 0, off).start()
+
+        def go1(off, carry, part=part):
+            first(lax.rem(re + off, n_re), re, part).start()
+            return carry
+
+        lax.fori_loop(1, n_re, go1, 0)
     loads[4].wait()
     for g in range(4):
         bz[:, :, g * 32 : g * 32 + 32] = bands[:, g // 2, g % 2 * 8 : g % 2 * 8 + 8, :]
@@ -290,13 +294,13 @@
     pick = ((iota((rows, 128), 0) // 4) == iota((rows, 128), 1)).astype(bf16)
     grid = lax.dot_general(pick, points.astype(bf16), NT, preferred_element_type=f32).astype(bf16)
 
-    def got1(off, carry):
-        first(re, lax.rem(re + off, n_re)).wait_recv()
+    def got1(off, carry, part=0):
+        first(re, lax.rem(re + off, n_re), part).wait_recv()
         return carry
 
     lax.fori_loop(1, n_re, got1, 0)
     depth = n_re * 16
-    lattice = X[:, :, 512:640].reshape(depth, 128)
+    lattice = X[:, :, 0:128].reshape(depth, 128)
     product = lax.dot_general(grid, lattice, NT, preferred_element_type=f32)
     ones = (iota((rows, 128), 1) == 67).astype(bf16)
     degen = lax.dot_general(ones, lattice, NT, preferred_element_type=f32)
@@ -305,23 +309,44 @@
     turn = (((col // 8) & 1) - (row & 1)).astype(f32) * 4.0
     same = ((row // 2) & 1) == (col & 1)
     phases = jnp.where(same, unit_cosine(product + turn) * (1.0 / degen), 0.0).astype(bf16)
-    for t in range(5):
-        lanes = slice(t * 128, t * 128 + 128)
-        bloch = dot16(phases, X[:, :, lanes].reshape(depth, 128))
-        S[:, :, lanes] = bloch.reshape(n_all, 8, 128).astype(bf16)
-
-    def second(to, frm):
+
+    def second(to, frm, part):
+        lanes = pl.ds(*CHUNKS[part])
         return pltpu.make_async_remote_copy(
-            src_ref=S.at[to], dst_ref=D.at[frm],
-            send_sem=send2.at[to], recv_sem=recv2.at[frm],
+            src_ref=S.at[to, :, lanes], dst_ref=D.at[frm, :, lanes],
+            send_sem=send2.at[part, to], recv_sem=recv2.at[part, frm],
             device_id=(lax.rem(to, n_re), to // n_re), device_id_type=MESH,
         )
 
-    def go2(off, carry):
-        second(lax.rem(me + off, n_all), me).start()
-        return carry
-
-    lax.fori_loop(1, n_all, go2, 0)
+    def sum_and_send(part):
+        start, count = CHUNKS[part]
+        for at in range(start, start + count, 128):
+            bloch = dot16(phases, X[:, :, at : at + 128].reshape(depth, 128))
+            S[:, :, at : at + 128] = bloch.reshape(n_all, 8, 128).astype(bf16)
+
+        def go2(off, carry):
+            second(lax.rem(me + off, n_all), me, part).start()
+            return carry
+
+        lax.fori_loop(1, n_all, go2, 0)
+
+    sum_and_send(0)
+
+    down = ((iota((256, 128), 0) & 31) == iota((256, 128), 1)).astype(f32)
+    lane = iota((32, 256), 1)
+    across = iota((32, 256), 0) == (lane // 128) * NB + (lane & 15)
+    flip = iota((32, 256), 0) == (1 - lane // 128) * NB + (lane & 15)
+    minus = jnp.where(lane < 128, -1.0, 1.0)
+    same_mode = iota((256, 256), 0) // 32 == (iota((256, 256), 1) // NB) % 8
+    right = []
+    for k in range(2):
+        tall = exact(down, unpack_bands(bz[re * 2 + k]), NT)
+        a = exact(tall, across.astype(f32))
+        b = exact(tall, jnp.where(flip, minus, 0.0))
+        right.append([split(jnp.where(same_mode, w, 0.0)) for w in (a, b)])
+
+    lax.fori_loop(1, n_re, functools.partial(got1, part=1), 0)
+    sum_and_send(1)
     D[me] = S[me]
 
     for off in range(1, n_kq):
@@ -340,62 +365,63 @@
         left.append(jnp.where(own, jnp.where(imag_in, real, -imag), 0.0))
     left_high, left_low = split(jnp.concatenate(left, axis=0))
     left_both = jnp.concatenate([left_high, left_low], axis=0)
-    down = ((iota((256, 128), 0) & 31) == iota((256, 128), 1)).astype(f32)
-    lane = iota((32, 256), 1)
-    across = iota((32, 256), 0) == (lane // 128) * NB + (lane & 15)
-    flip = iota((32, 256), 0) == (1 - lane // 128) * NB + (lane & 15)
-    minus = jnp.where(lane < 128, -1.0, 1.0)
-    same_mode = iota((256, 256), 0) // 32 == (iota((256, 256), 1) // NB) % 8
-    right = []
-    for k in range(2):
-        tall = exact(down, unpack_bands(bz[re * 2 + k]), NT)
-        a = exact(tall, across.astype(f32))
-        b = exact(tall, jnp.where(flip, minus, 0.0))
-        right.append([split(jnp.where(same_mode, w, 0.0)) for w in (a, b)])
-
-    def got2(off, carry):
-        second(me, lax.rem(me + off, n_all)).wait_recv()
-        return carry
-
-    lax.fori_loop(1, n_all, got2, 0)
-    data = D[...].astype(f32).reshape(n_all * 8, LANES).astype(bf16)
-    both = dot16(left_both, data)
-    summed = both[:128] + both[128:]
-    groups = [
-        summed[:, 0:256],
-        summed[:, 256:512],
-        jnp.concatenate([summed[:, 512:640], jnp.zeros((128, 128), f32)], axis=1),
+    pieces = [[{} for c in range(2)] for q in range(2)]
+    for part, (start, count) in enumerate(CHUNKS):
+
+        def got2(off, carry, part=part):
+            second(me, lax.rem(me + off, n_all), part).wait_recv()
+            return carry
+
+        lax.fori_loop(1, n_all, got2, 0)
+        data = D[:, :, start : start + count].astype(f32).reshape(n_all * 8, count).astype(bf16)
+        both = dot16(left_both, data)
+        summed = both[:128] + both[128:]
+        if part == 0:
+            groups = {
+                0: summed[:, 128:384],
+                2: jnp.concatenate([summed[:, 0:128], jnp.zeros((128, 128), f32)], axis=1),
+            }
+        else:
+            groups = {1: summed}
+        for k in range(2):
+            total = None
+            for c in range(2):
+                x = jnp.concatenate(
+                    [
+                        g[((k * 2 + q) * 2 + c) * NB : ((k * 2 + q) * 2 + c + 1) * NB]
+                        for g in groups.values()
+                        for q in range(2)
+                    ],
+                    axis=0,
+                )
+                high, low = split(x)
+                w_high, w_low = right[k][c]
+                term = dot16(high, w_high) + dot16(low, w_high) + dot16(high, w_low)
+                total = term if total is None else total + term
+            for c in range(2):
+                turned = group_swap(total[:, c * 128 : c * 128 + 128])
+                for n, g in enumerate(groups):
+                    for q in range(2):
+                        for h in range(2):
+                            at = (n * 2 + q) * NB + h * 8
+                            pieces[q][c][g, k, h] = turned[at : at + 8]
+    values = [
+        [
+            jnp.concatenate(
+                [
+                    jnp.concatenate([pieces[q][c][g, k, h] for g in range(3)], axis=0)
+                    for k in range(2)
+                    for h in range(2)
+                ],
+                axis=1,
+            )
+            for c in range(2)
+        ]
+        for q in range(2)
     ]
-    values = [[None, None], [None, None]]
-    for k in range(2):
-        total = None
-        for c in range(2):
-            x = jnp.concatenate(
-                [g[((k * 2 + q) * 2 + c) * NB : ((k * 2 + q) * 2 + c + 1) * NB] for g in groups for q in range(2)],
-                axis=0,
-            )
-            high, low = split(x)
-            w_high, w_low = right[k][c]
-            term = dot16(high, w_high) + dot16(low, w_high) + dot16(high, w_low)
-            total = term if total is None else total + term
-        for c in range(2):
-            turned = group_swap(total[:, c * 128 : c * 128 + 128])
-            for q in range(2):
-                values[q][c] = (values[q][c] or []) + [
-                    jnp.concatenate(
-                        [
-                            jnp.concatenate(
-                                [turned[(g * 2 + q) * NB + h * 8 : (g * 2 + q) * NB + h * 8 + 8] for g in range(3)],
-                                axis=0,
-                            )
-                            for h in range(2)
-                        ],
-                        axis=1,
-                    )
-                ]
     for q in range(2):
-        xr = jnp.concatenate(values[q][0], axis=1)[:M]
-        xi = jnp.concatenate(values[q][1], axis=1)[:M]
+        xr = values[q][0][:M]
+        xi = values[q][1][:M]
         er, ei = mode[q, :, 0, :], mode[q, :, 1, :]
         yr = exact(er, xr, TN) - exact(ei, xi, TN)
         yi = exact(er, xi, TN) + exact(ei, xr, TN)
@@ -408,17 +434,18 @@
         swap(kp, KP, 0, off).wait_send()
         swap(bz, BZ, 1, off).wait_send()
 
-    def sent1(off, carry):
-        first(lax.rem(re + off, n_re), re).wait_send()
-        return carry
-
-    lax.fori_loop(1, n_re, sent1, 0)
-
-    def sent2(off, carry):
-        second(lax.rem(me + off, n_all), me).wait_send()
-        return carry
-
-    lax.fori_loop(1, n_all, sent2, 0)
+    for part in range(2):
+
+        def sent1(off, carry, part=part):
+            first(lax.rem(re + off, n_re), re, part).wait_send()
+            return carry
+
+        def sent2(off, carry, part=part):
+            second(lax.rem(me + off, n_all), me, part).wait_send()
+            return carry
+
+        lax.fori_loop(1, n_re, sent1, 0)
+        lax.fori_loop(1, n_all, sent2, 0)
 
 
 def fused(n_re, n_kq, couplings, re_vectors, degeneracy, kpoints, plus_index, mode_vectors, band_vectors):
@@ -448,10 +475,10 @@
             pltpu.VMEM((k_dev, 8, 128), f32),
             pltpu.VMEM((8, 128), f32),
             pltpu.SemaphoreType.DMA((7,)),
-            pltpu.SemaphoreType.DMA((n_re,)),
-            pltpu.SemaphoreType.DMA((n_re,)),
-            pltpu.SemaphoreType.DMA((n_all,)),
-            pltpu.SemaphoreType.DMA((n_all,)),
+            pltpu.SemaphoreType.DMA((2, n_re)),
+            pltpu.SemaphoreType.DMA((2, n_re)),
+            pltpu.SemaphoreType.DMA((2, n_all)),
+            pltpu.SemaphoreType.DMA((2, n_all)),
             pltpu.SemaphoreType.DMA((2, n_kq)),
             pltpu.SemaphoreType.DMA((2, n_kq)),
         ],

time: 29.1 us -> 30.6 us (1.052)
  Pallas kernels: 27.4 us -> 28.9 us
    pallas_call x1, Pallas kernels: 27.4 us -> 28.9 us  [fused(): pl.pallas_call(functools.partial(kernel, n_re, n_kq), out_shape=jax.Shape...]
where the time goes in v3:
time: 30.6 us; the launch traced here: 30.5 us
  Pallas kernels  28.9 us (94%)
  local copies, waits for them, and re-layouts  1.58 us (5%)
    pallas_call x1, Pallas kernels, fused(): pl.pallas_call(functools.partial(kernel, n_re, n_kq), out_shape=jax.Shape...  28.9 us
    unnamed x1, local copies, waits for them, and re-layouts  1.58 us

profile of v3, /device:TPU:0, one launch (start us, length us, event | category | flops | bytes accessed | tf_op | source)
XLA Modules:
  0.0 30.5 jit_solution(11840703904246858939)
XLA Ops:
  0.0 28.9 %shard_map.73 = f32[1,1,72,512]{3,2,1,0:T(8,128)} custom-call(bf16[2,4,18,2,1024]{4,3,2,1,0:T(2,128)(2,1)} %bitcast.5, s32[4,3]{1,0:T(4,128)} %rvec_any.1, s32[4]{0:T(128)} %degen_any.1, s32[3,32]{1,0:T(4,128)} %bitcast.8, s32[2,32]{1,0:T(2,128)} %bitcast.9, f32[2,18,2,18]{3,2,1,0:T(2,128)} %bitcast.7, f32[32,2,16,32]{3,2,1,0:T(8,128)} %bitcast.6), custom_call_target="tpu_custom_call" | custom-call | tf_op jit(solution)/shard_map/pallas_call | solution.py:455
  28.9 1.6 %copy.9 = f32[1,1,72,512]{3,2,1,0:T(8,128)} copy(f32[1,1,72,512]{3,2,1,0:T(8,128)} %shard_map.73) | data formatting | bytes 294912

commit v4 on v2

--- a/solution.py
+++ b/solution.py
@@ -204,14 +204,11 @@
         load.start()
     barrier = pltpu.get_barrier_semaphore()
 
-    def hello(off, carry):
+    for off in range(1, n_all):
         to = lax.rem(me + off, n_all)
         pl.semaphore_signal(
             barrier, inc=1, device_id=(lax.rem(to, n_re), to // n_re), device_id_type=MESH
         )
-        return carry
-
-    lax.fori_loop(1, n_all, hello, 0)
 
     for n in range(4):
         loads[n].wait()
@@ -241,7 +238,7 @@
     def first(to, frm):
         return pltpu.make_async_remote_copy(
             src_ref=Y.at[to], dst_ref=X.at[frm],
-            send_sem=send1.at[to], recv_sem=recv1.at[frm],
+            send_sem=send1, recv_sem=recv1,
             device_id=(to, kq), device_id_type=MESH,
         )
 
@@ -264,11 +261,8 @@
     for off in range(1, n_kq):
         swap(kp, KP, 0, off).start()
 
-    def go1(off, carry):
+    for off in range(1, n_re):
         first(lax.rem(re + off, n_re), re).start()
-        return carry
-
-    lax.fori_loop(1, n_re, go1, 0)
     loads[4].wait()
     for g in range(4):
         bz[:, :, g * 32 : g * 32 + 32] = bands[:, g // 2, g % 2 * 8 : g % 2 * 8 + 8, :]
@@ -290,11 +284,11 @@
     pick = ((iota((rows, 128), 0) // 4) == iota((rows, 128), 1)).astype(bf16)
     grid = lax.dot_general(pick, points.astype(bf16), NT, preferred_element_type=f32).astype(bf16)
 
-    def got1(off, carry):
-        first(re, lax.rem(re + off, n_re)).wait_recv()
-        return carry
-
-    lax.fori_loop(1, n_re, got1, 0)
+    every1 = pltpu.make_async_remote_copy(
+        src_ref=Y.at[0 : n_re - 1], dst_ref=X.at[0 : n_re - 1], send_sem=send1, recv_sem=recv1,
+        device_id=(lax.rem(re + 1, n_re), kq), device_id_type=MESH,
+    )
+    every1.wait_recv()
     depth = n_re * 16
     lattice = X[:, :, 512:640].reshape(depth, 128)
     product = lax.dot_general(grid, lattice, NT, preferred_element_type=f32)
@@ -313,15 +307,12 @@
     def second(to, frm):
         return pltpu.make_async_remote_copy(
             src_ref=S.at[to], dst_ref=D.at[frm],
-            send_sem=send2.at[to], recv_sem=recv2.at[frm],
+            send_sem=send2, recv_sem=recv2,
             device_id=(lax.rem(to, n_re), to // n_re), device_id_type=MESH,
         )
 
-    def go2(off, carry):
+    for off in range(1, n_all):
         second(lax.rem(me + off, n_all), me).start()
-        return carry
-
-    lax.fori_loop(1, n_all, go2, 0)
     D[me] = S[me]
 
     for off in range(1, n_kq):
@@ -353,11 +344,11 @@
         b = exact(tall, jnp.where(flip, minus, 0.0))
         right.append([split(jnp.where(same_mode, w, 0.0)) for w in (a, b)])
 
-    def got2(off, carry):
-        second(me, lax.rem(me + off, n_all)).wait_recv()
-        return carry
-
-    lax.fori_loop(1, n_all, got2, 0)
+    every2 = pltpu.make_async_remote_copy(
+        src_ref=S.at[0 : n_all - 1], dst_ref=D.at[0 : n_all - 1], send_sem=send2, recv_sem=recv2,
+        device_id=(lax.rem(re + 1, n_re), kq), device_id_type=MESH,
+    )
+    every2.wait_recv()
     data = D[...].astype(f32).reshape(n_all * 8, LANES).astype(bf16)
     both = dot16(left_both, data)
     summed = both[:128] + both[128:]
@@ -408,17 +399,8 @@
         swap(kp, KP, 0, off).wait_send()
         swap(bz, BZ, 1, off).wait_send()
 
-    def sent1(off, carry):
-        first(lax.rem(re + off, n_re), re).wait_send()
-        return carry
-
-    lax.fori_loop(1, n_re, sent1, 0)
-
-    def sent2(off, carry):
-        second(lax.rem(me + off, n_all), me).wait_send()
-        return carry
-
-    lax.fori_loop(1, n_all, sent2, 0)
+    every1.wait_send()
+    every2.wait_send()
 
 
 def fused(n_re, n_kq, couplings, re_vectors, degeneracy, kpoints, plus_index, mode_vectors, band_vectors):
@@ -448,10 +430,10 @@
             pltpu.VMEM((k_dev, 8, 128), f32),
             pltpu.VMEM((8, 128), f32),
             pltpu.SemaphoreType.DMA((7,)),
-            pltpu.SemaphoreType.DMA((n_re,)),
-            pltpu.SemaphoreType.DMA((n_re,)),
-            pltpu.SemaphoreType.DMA((n_all,)),
-            pltpu.SemaphoreType.DMA((n_all,)),
+            pltpu.SemaphoreType.DMA,
+            pltpu.SemaphoreType.DMA,
+            pltpu.SemaphoreType.DMA,
+            pltpu.SemaphoreType.DMA,
             pltpu.SemaphoreType.DMA((2, n_kq)),
             pltpu.SemaphoreType.DMA((2, n_kq)),
         ],

time: 29.1 us -> 27.7 us (0.952)
  Pallas kernels: 27.4 us -> 26 us
    pallas_call x1, Pallas kernels: 27.4 us -> 26 us  [fused(): pl.pallas_call(functools.partial(kernel, n_re, n_kq), out_shape=jax.Shape...]
where the time goes in v4:
time: 27.7 us; the launch traced here: 27.6 us
  Pallas kernels  26 us (94%)
  local copies, waits for them, and re-layouts  1.58 us (6%)
    pallas_call x1, Pallas kernels, fused(): pl.pallas_call(functools.partial(kernel, n_re, n_kq), out_shape=jax.Shape...  26 us
    unnamed x1, local copies, waits for them, and re-layouts  1.58 us

profile of v4, /device:TPU:0, one launch (start us, length us, event | category | flops | bytes accessed | tf_op | source)
XLA Modules:
  0.0 27.6 jit_solution(13662334599041358396)
XLA Ops:
  0.0 26.0 %shard_map.73 = f32[1,1,72,512]{3,2,1,0:T(8,128)} custom-call(bf16[2,4,18,2,1024]{4,3,2,1,0:T(2,128)(2,1)} %bitcast.5, s32[4,3]{1,0:T(4,128)} %rvec_any.1, s32[4]{0:T(128)} %degen_any.1, s32[3,32]{1,0:T(4,128)} %bitcast.8, s32[2,32]{1,0:T(2,128)} %bitcast.9, f32[2,18,2,18]{3,2,1,0:T(2,128)} %bitcast.7, f32[32,2,16,32]{3,2,1,0:T(8,128)} %bitcast.6), custom_call_target="tpu_custom_call" | custom-call | tf_op jit(solution)/shard_map/pallas_call | solution.py:410
  26.0 1.6 %copy.9 = f32[1,1,72,512]{3,2,1,0:T(8,128)} copy(f32[1,1,72,512]{3,2,1,0:T(8,128)} %shard_map.73) | data formatting | bytes 294912

commit v5 on v4

--- a/solution.py
+++ b/solution.py
@@ -311,8 +311,12 @@
             device_id=(lax.rem(to, n_re), to // n_re), device_id_type=MESH,
         )
 
-    for off in range(1, n_all):
-        second(lax.rem(me + off, n_all), me).start()
+    offsets = list(range(n_re - 1, 0, -1))
+    for off in offsets + [0]:
+        for turn in range(n_kq):
+            if off or turn:
+                to = lax.rem(kq + turn, n_kq) * n_re + jnp.bitwise_xor(re, off)
+                second(to, me).start()
     D[me] = S[me]
 
     for off in range(1, n_kq):

time: 27.7 us -> 27.2 us (0.982)
  Pallas kernels: 26 us -> 25.4 us
    pallas_call x1, Pallas kernels: 26 us -> 25.4 us  [fused(): pl.pallas_call(functools.partial(kernel, n_re, n_kq), out_shape=jax.Shape...]
where the time goes in v5:
time: 27.2 us; the launch traced here: 27 us
  Pallas kernels  25.4 us (93%)
  local copies, waits for them, and re-layouts  1.58 us (6%)
    pallas_call x1, Pallas kernels, fused(): pl.pallas_call(functools.partial(kernel, n_re, n_kq), out_shape=jax.Shape...  25.4 us
    unnamed x1, local copies, waits for them, and re-layouts  1.58 us

profile of v5, /device:TPU:0, one launch (start us, length us, event | category | flops | bytes accessed | tf_op | source)
XLA Modules:
  0.0 27.0 jit_solution(11467281281687170235)
XLA Ops:
  0.0 25.4 %shard_map.73 = f32[1,1,72,512]{3,2,1,0:T(8,128)} custom-call(bf16[2,4,18,2,1024]{4,3,2,1,0:T(2,128)(2,1)} %bitcast.5, s32[4,3]{1,0:T(4,128)} %rvec_any.1, s32[4]{0:T(128)} %degen_any.1, s32[3,32]{1,0:T(4,128)} %bitcast.8, s32[2,32]{1,0:T(2,128)} %bitcast.9, f32[2,18,2,18]{3,2,1,0:T(2,128)} %bitcast.7, f32[32,2,16,32]{3,2,1,0:T(8,128)} %bitcast.6), custom_call_target="tpu_custom_call" | custom-call | tf_op jit(solution)/shard_map/pallas_call | solution.py:414
  25.5 1.6 %copy.9 = f32[1,1,72,512]{3,2,1,0:T(8,128)} copy(f32[1,1,72,512]{3,2,1,0:T(8,128)} %shard_map.73) | data formatting | bytes 294912
